TPU v7x, 32 devices: a whole 2x2x4 slice. The times are simulated.
32 devices in a mesh: groups: 2 (over y), expert: 4 (over x, core), tensor: 4 (over z).
Axes of the slice: x: 2, y: 2, z: 4, core: 2. Of those that a mesh axis runs over, the one named last changes fastest.
Arguments:
- tokens: bfloat16 [1536, 3072], P(('groups', 'expert'), 'tensor'), parts along dimension 0, may hold values from -6 to 6
- routes: int32 [1536, 2], P('groups'), parts along dimension 0, may hold values from 0 to 3, all different within a row; in each aligned block of 192 rows (0 to 191, 192 to 383, ...) at most 144 rows name the same one
- probs: float32 [1536, 2], P(('groups', 'expert')), parts along dimension 0, may hold values from 0.2 to 1
- request_adapter: int32 [16], P('groups'), parts along dimension 0, may hold values from 0 to 1
- gate_quant_levels: bfloat16 [4, 3072, 8192], P('expert', None, 'tensor'), may hold values from -127 to 127, as said below
- up_quant_levels: bfloat16 [4, 3072, 8192], P('expert', None, 'tensor'), may hold values from -127 to 127, as said below
- down_quant_levels: bfloat16 [4, 8192, 3072], P('expert', 'tensor'), may hold values from -127 to 127, as said below
- gate_column_scale: float32 [4, 8192], P('expert', 'tensor'), may hold values from 0 to 1, as said below
- up_column_scale: float32 [4, 8192], P('expert', 'tensor'), may hold values from 0 to 1, as said below
- down_column_scale: float32 [4, 3072], P('expert'), may hold values from 0 to 1, as said below
- adapter_input_maps: bfloat16 [4, 3072, 256], P('expert', 'tensor'), may hold values from -0.109375 to 0.109375
- adapter_output_maps: bfloat16 [4, 2, 128, 8192], P('expert', None, None, 'tensor'), may hold values from -0.75 to 0.75
Outputs:
- moe_output: bfloat16 [1536, 3072], P(('groups', 'expert'), 'tensor'), parts along dimension 0
There are 2 independent parts, one for each index of `groups`. A program takes and returns all parts, laid end to end along the dimension named above; an argument that names none is the same for every part. Nothing has to cross between parts.
Inputs may be any that keep to these rules, and one draw needn't show every extreme that they name: `routes`: the two experts of a token differ. In each aligned block of 192 rows (the rows of one index of expert) no expert is named by more than 144 rows, a bound that some block reaches. `gate_quant_levels`: whole numbers. `up_quant_levels`: whole numbers. `down_quant_levels`: whole numbers. `gate_column_scale`: Positive. `up_column_scale`: Positive. `down_column_scale`: Positive.
All inputs are finite; a program needn't handle non-finite values.
Results may differ from a plain program's by a relative error of at most 0.011.
Values may be sent and summed in bfloat16 or wider, within the bound.
A program may use at most 128 MiB of HBM per device.

v0:
```python
import jax
import jax.numpy as jnp
from jax import lax
from jax.sharding import PartitionSpec as P

ADAPTER_RANK = 64
ADAPTER_COUNT = 2


def slot_positions(routes_flat, expert_count):
    experts_range = jnp.arange(expert_count, dtype=jnp.int32)
    onehot = (routes_flat[..., None] == experts_range).astype(jnp.int32)
    earlier = jnp.cumsum(onehot, axis=1) - onehot
    return jnp.sum(onehot * earlier, axis=-1)


def slot_sources(routes_flat, positions, expert_count, capacity, tok_dev):
    blocks = routes_flat.shape[0]
    entries = routes_flat.shape[1]
    experts_range = jnp.arange(expert_count, dtype=jnp.int32)
    slot_range = jnp.arange(capacity, dtype=jnp.int32)
    matched = (
        (routes_flat[None, :, None, :] == experts_range[:, None, None, None])
        & (positions[None, :, None, :] == slot_range[None, None, :, None])
    ).astype(jnp.int32)
    source_row = (
        jnp.arange(blocks, dtype=jnp.int32)[:, None] * tok_dev
        + jnp.arange(entries, dtype=jnp.int32)[None, :] // 2
    )
    found = jnp.sum(matched, axis=-1)
    return jnp.sum(matched * source_row[None, :, None, :], axis=-1) + (1 - found) * (
        blocks * tok_dev
    )


def slot_adapters(routes_flat, positions, entry_adapter, expert_index, capacity):
    slot_range = jnp.arange(capacity, dtype=jnp.int32)
    matched = (
        (routes_flat == expert_index)[:, None, :]
        & (positions[:, None, :] == slot_range[None, :, None])
    ).astype(jnp.float32)
    adapter_hot = (entry_adapter[..., None] == jnp.arange(ADAPTER_COUNT, dtype=jnp.int32)).astype(
        jnp.float32
    )
    return jnp.einsum("bsj,bja->bsa", matched, adapter_hot)


def body(
    tokens,
    routes,
    probs,
    request_adapter,
    gate_quant_levels,
    up_quant_levels,
    down_quant_levels,
    gate_column_scale,
    up_column_scale,
    down_column_scale,
    adapter_input_maps,
    adapter_output_maps,
):
    expert_count = lax.axis_size("expert")
    expert_index = lax.axis_index("expert")
    tok_dev = tokens.shape[0]
    width_part = tokens.shape[1]
    capacity = max(2, min(tok_dev, 3 * (2 * tok_dev // expert_count) // 2))
    slot_count = expert_count * capacity
    requests = request_adapter.shape[0]
    request_length = routes.shape[0] // requests
    routes_flat = routes.reshape(expert_count, 2 * tok_dev)
    positions = slot_positions(routes_flat, expert_count)
    entry_token = (
        jnp.arange(expert_count, dtype=jnp.int32)[:, None] * tok_dev
        + jnp.arange(2 * tok_dev, dtype=jnp.int32)[None, :] // 2
    )
    entry_request = entry_token // request_length
    request_hot = (entry_request[..., None] == jnp.arange(requests, dtype=jnp.int32)).astype(
        jnp.int32
    )
    entry_adapter = jnp.sum(request_hot * request_adapter, axis=-1)
    table = slot_adapters(routes_flat, positions, entry_adapter, expert_index, capacity).reshape(
        -1, ADAPTER_COUNT
    )
    own_routes = lax.dynamic_slice_in_dim(routes_flat, expert_index, 1, 0)[0]
    own_positions = lax.dynamic_slice_in_dim(positions, expert_index, 1, 0)[0]
    sources = slot_sources(
        own_routes[None], own_positions[None], expert_count, capacity, tok_dev
    ).reshape(-1)
    gate_weight = gate_quant_levels[0]
    up_weight = up_quant_levels[0]
    adapter_row_block = adapter_input_maps[0]
    padded = jnp.concatenate([tokens, jnp.zeros((1, width_part), jnp.bfloat16)], axis=0)
    outgoing = jnp.take(padded, sources, axis=0).reshape(expert_count, capacity, width_part)
    arrived = lax.all_to_all(outgoing, "expert", split_axis=0, concat_axis=0, tiled=True).reshape(
        -1, width_part
    )
    piece = lax.all_gather(arrived, "tensor", axis=1, tiled=True)
    gate_next = jnp.dot(piece, gate_weight, preferred_element_type=jnp.float32)
    up_next = jnp.dot(piece, up_weight, preferred_element_type=jnp.float32)
    mixed = jnp.dot(arrived, adapter_row_block, preferred_element_type=jnp.float32)
    gate_plain_term = gate_next * gate_column_scale[0]
    up_plain_term = up_next * up_column_scale[0]
    selected = jnp.sum(
        mixed.reshape(-1, 2, ADAPTER_COUNT, ADAPTER_RANK) * table[:, None, :, None], axis=2
    ).reshape(-1, 2 * ADAPTER_RANK)
    selected = lax.psum(selected, "tensor")
    latent = selected.astype(jnp.bfloat16).reshape(-1, 2, ADAPTER_RANK)
    spread_latent = (latent[:, :, None, :] * table.astype(jnp.bfloat16)[:, None, :, None]).reshape(
        -1, 2, ADAPTER_COUNT * ADAPTER_RANK
    )
    gate_values = gate_plain_term + jnp.dot(
        spread_latent[:, 0], adapter_output_maps[0, 0], preferred_element_type=jnp.float32
    )
    upper_values = up_plain_term + jnp.dot(
        spread_latent[:, 1], adapter_output_maps[0, 1], preferred_element_type=jnp.float32
    )
    hidden = (jax.nn.silu(gate_values) * upper_values).astype(jnp.bfloat16)
    down_weight = down_quant_levels[0]
    down_gain = down_column_scale[0]
    term = lax.dot_general(
        down_weight, hidden, (((0,), (1,)), ((), ())), preferred_element_type=jnp.float32
    )
    summed = lax.psum_scatter(
        (term * down_gain[:, None]).astype(jnp.bfloat16), "tensor", scatter_dimension=0, tiled=True
    )
    returned = lax.all_to_all(
        summed.reshape(width_part, expert_count, capacity),
        "expert",
        split_axis=1,
        concat_axis=1,
        tiled=True,
    ).reshape(width_part, slot_count)
    targets = own_routes * capacity + own_positions
    match = (
        (jnp.arange(slot_count, dtype=jnp.int32)[:, None] == targets[None, :])
        .astype(jnp.float32)
        .reshape(slot_count, tok_dev, 2)
    )
    combine = jnp.sum(match * probs[None, :, :], axis=2)
    output = lax.dot_general(
        combine,
        returned.astype(jnp.float32),
        (((0,), (1,)), ((), ())),
        precision=lax.Precision.HIGHEST,
        preferred_element_type=jnp.float32,
    )
    return output.astype(jnp.bfloat16)


def solution(mesh):
    return jax.shard_map(
        body,
        mesh=mesh,
        in_specs=(
            P(("groups", "expert"), "tensor"),
            P("groups", None),
            P(("groups", "expert"), None),
            P("groups"),
            P("expert", None, "tensor"),
            P("expert", None, "tensor"),
            P("expert", "tensor", None),
            P("expert", "tensor"),
            P("expert", "tensor"),
            P("expert", None),
            P("expert", "tensor", None),
            P("expert", None, None, "tensor"),
        ),
        out_specs=P(("groups", "expert"), "tensor"),
        check_vma=False,
    )
```

profile of v0, /device:TPU:0, one launch (start us, length us, event | category | flops | bytes accessed | tf_op | source)
XLA Modules:
  0.0 246.5 jit_solution(17898541615515950724)
XLA Ops:
  6.5 0.9 copy.27
  7.4 0.3 eq.130
  7.7 0.2 reshape.282
  7.9 4.8 %reduce-window.6 = s32[4,4,3,128]{3,2,1,0:T(4,128)S(1)} reduce-window(s32[4,4,3,128]{3,2,1,0:T(4,128)S(1)} %fusion.27, s32[]{:T(128)} %constant.58.clone.1), window={size=1x1x1x128 pad=0_0x0_0x0_0x127_0}, to_apply=%region_0.0 | reduce-window | flops 780288 | bytes 49156 | tf_op jit(solution)/shard_map/reduce-window
  12.8 0.1 slice.26
  12.9 0.2 copy.29
  13.0 0.1 copy.30
  13.1 0.1 broadcast_add_fusion
  13.4 0.4 fusion.15
  13.8 0.1 add.102
  13.9 1.0 concatenate.3
  14.9 2.9 %gather_fusion = bf16[576,768]{1,0:T(8,128)(2,1)S(1)} fusion(bf16[193,768]{1,0:T(8,128)(2,1)S(1)} %concatenate.3, s32[1024]{0:T(1024)S(1)} %pad_clamp_fusion), kind=kCustom, calls=%fused_computation | custom fusion | bytes 1771776 | tf_op jit(solution)/shard_map/jit(_take)/gather | solution.py:93
  17.8 0.2 broadcast_select_fusion
  18.0 17.0 %all_to_all.10 = bf16[4,144,768]{2,1,0:T(8,128)(2,1)} all-to-all(bf16[4,144,768]{2,1,0:T(8,128)(2,1)S(1)} %broadcast_select_fusion), channel_id=1, replica_groups=mesh['groups'=2,'expert'=4,'tensor'=4] {'expert'}, dimensions={0} | all-to-all | bytes 1769472 | tf_op jit(solution)/shard_map/all_to_all | solution.py:94
  35.0 0.1 add_select_fusion
  35.1 0.1 select_reduce_fusion.1
  35.2 0.3 fusion.17
  35.5 0.1 mul.147
  35.6 0.2 copy.32
  35.8 1.7 fusion.13
  37.5 35.8 %all-reduce.2 = bf16[576,128]{0,1:T(8,128)(2,1)S(1)} all-reduce(f32[576,128]{0,1:T(8,128)S(1)} %bitcast.86), channel_id=1, replica_groups=mesh['groups'=2,'expert'=4,'tensor'=4] {'tensor'}, use_global_device_ids=true, to_apply=%region_8.9 | all-reduce | flops 73728 | bytes 442368 | tf_op jit(solution)/shard_map/psum | solution.py:106
  73.5 2.9 %fusion.19 = f32[576,2048]{1,0:T(8,128)} fusion(bf16[1,2,128,2048]{3,2,1,0:T(8,128)(2,1)S(1)} %copy-done, bf16[576,2,128]{0,2,1:T(8,128)(2,1)S(1)} %bitcast_multiply_fusion), kind=kOutput, calls=%fused_computation.23 | convolution fusion | flops 301989888 | bytes 5406720 | tf_op jit(solution)/shard_map/dot_general | solution.py:114
  76.4 3.0 %fusion.21 = f32[576,2048]{1,0:T(8,128)} fusion(bf16[1,2,128,2048]{3,2,1,0:T(8,128)(2,1)S(1)} %copy-done, bf16[576,2,128]{0,2,1:T(8,128)(2,1)S(1)} %bitcast_multiply_fusion), kind=kOutput, calls=%fused_computation.25 | convolution fusion | flops 301989888 | bytes 5406720 | tf_op jit(solution)/shard_map/dot_general | solution.py:111
  79.4 33.4 %all-gather.2.cloned.1.call-done = bf16[576,3072]{1,0:T(8,128)(2,1)} async-done(((bf16[576,768]{1,0:T(8,128)(2,1)}), bf16[576,3072]{1,0:T(8,128)(2,1)}) %all-gather.2.cloned.1.call-update) | async-done | bytes 3538960 | tf_op jit(solution)/shard_map/all_gather | solution.py:97
  112.8 14.6 %fusion.2 = f32[576,2048]{1,0:T(8,128)} fusion(bf16[576,3072]{1,0:T(8,128)(2,1)} %all-gather.2.cloned.1.call-done, bf16[1,3072,2048]{2,1,0:T(8,128)(2,1)} %param.17), kind=kOutput, calls=%fused_computation.3 | convolution fusion | flops 7247757312 | bytes 20840448 | tf_op jit(solution)/shard_map/dot_general | solution.py:99
  127.3 28.4 %fusion.8 = bf16[3072,576]{0,1:T(8,128)(2,1)} fusion(bf16[1,2048,3072]{2,1,0:T(8,128)(2,1)} %param.18, f32[3072]{0:T(1024)S(1)} %bitcast.87, f32[576,2048]{1,0:T(8,128)} %fusion.19, f32[576,2048]{1,0:T(8,128)} %fusion.2, f32[576,2048]{1,0:T(8,128)} %fusion.21, bf16[576,3072]{1,0:T(8,128)(2,1)S(1)} %copy-done.4, bf16[1,3072,2048]{2,1,0:T(8,128)(2,1)} %param.16, ...), kind=kOutput, calls=%fused_computation.9 | convolution fusion | flops 14510850048 | bytes 46428160 | tf_op jit(solution)/shard_map/dot_general | solution.py:120
  155.8 66.1 %reduce-scatter.2.cloned.1.call-done = bf16[768,576]{0,1:T(8,128)(2,1)} async-done(((bf16[3072,576]{0,1:T(8,128)(2,1)}), bf16[768,576]{0,1:T(8,128)(2,1)}) %reduce-scatter.2.cloned.1.call-update) | async-done | bytes 884752 | tf_op jit(solution)/shard_map/reduce_scatter | solution.py:123
  221.9 3.5 %all-to-all-start.1 = ((bf16[768,4,144]{0,2,1:T(8,128)(2,1)}), bf16[768,4,144]{0,2,1:T(8,128)(2,1)S(1)}, u32[]{:S(2)}, u32[]{:S(2)}) async-start(bf16[768,4,144]{0,2,1:T(8,128)(2,1)} %bitcast.82), calls=%async_computation.2 | async-start | bytes 1769472 | tf_op jit(solution)/shard_map/all_to_all | solution.py:126
  225.4 0.1 eq.134
  225.6 0.2 select_reduce_fusion
  225.8 12.2 %all-to-all-done.1 = bf16[768,4,144]{0,2,1:T(8,128)(2,1)S(1)} async-done(((bf16[768,4,144]{0,2,1:T(8,128)(2,1)}), bf16[768,4,144]{0,2,1:T(8,128)(2,1)S(1)}, u32[]{:S(2)}, u32[]{:S(2)}) %all-to-all-start.1) | async-done | bytes 884768 | tf_op jit(solution)/shard_map/all_to_all | solution.py:126
  238.0 1.6 convolution_convert_fusion
  (35 shorter events, 0.5 us)
Async XLA Ops:
  6.5 106.2 %all-gather.2.cloned.1.call-start = ((), (), s32[]{:S(2)}) async-start(), calls=%async_computation.3 | async-start | bytes 4423680 | tf_op jit(solution)/shard_map/all_gather | solution.py:97
  14.9 20.2 %copy-start.3 = (s32[8]{0:T(128)S(1)}, s32[8]{0:T(128)}, u32[]{:S(2)}) copy-start(s32[8]{0:T(128)} %param.15) | copy-start | bytes 100
  14.9 20.7 %copy-start.1 = (bf16[1,768,256]{2,1,0:T(8,128)(2,1)S(1)}, bf16[1,768,256]{2,1,0:T(8,128)(2,1)}, u32[]{:S(2)}) copy-start(bf16[1,768,256]{2,1,0:T(8,128)(2,1)} %param.22) | copy-start | bytes 1179652
  17.8 55.6 %copy-start = (bf16[1,2,128,2048]{3,2,1,0:T(8,128)(2,1)S(1)}, bf16[1,2,128,2048]{3,2,1,0:T(8,128)(2,1)}, u32[]{:S(2)}) copy-start(bf16[1,2,128,2048]{3,2,1,0:T(8,128)(2,1)} %param.23) | copy-start | bytes 3145732
  35.0 186.9 %reduce-scatter.2.cloned.1.call-start = ((), (), s32[]{:S(2)}) async-start(), calls=%async_computation.4 | async-start | bytes 4423680 | tf_op jit(solution)/shard_map/reduce_scatter | solution.py:123
  79.4 48.0 %copy-start.5 = (f32[1,3072]{1,0:T(1,128)S(1)}, f32[1,3072]{1,0:T(1,128)}, u32[]{:S(2)}) copy-start(f32[1,3072]{1,0:T(1,128)} %param.21) | copy-start | bytes 36868
  112.8 14.6 %copy-start.4 = (bf16[576,3072]{1,0:T(8,128)(2,1)S(1)}, bf16[576,3072]{1,0:T(8,128)(2,1)}, u32[]{:S(2)}) copy-start(bf16[576,3072]{1,0:T(8,128)(2,1)} %all-gather.2.cloned.1.call-done) | copy-start | bytes 10616836
  155.7 69.9 %copy-start.2 = (f32[192,2]{0,1:T(2,128)S(1)}, f32[192,2]{0,1:T(2,128)}, u32[]{:S(2)}) copy-start(f32[192,2]{0,1:T(2,128)} %param.14) | copy-start | bytes 4612
  221.9 16.2 %all-to-all-start.1 = ((bf16[768,4,144]{0,2,1:T(8,128)(2,1)}), bf16[768,4,144]{0,2,1:T(8,128)(2,1)S(1)}, u32[]{:S(2)}, u32[]{:S(2)}) async-start(bf16[768,4,144]{0,2,1:T(8,128)(2,1)} %bitcast.82), calls=%async_computation.2 | async-start | bytes 1769472 | tf_op jit(solution)/shard_map/all_to_all | solution.py:126
Sparse Core Ops, SparseCore 0:
  35.1 77.6 all-gather.1
  155.9 65.9 reduce-scatter.1
where the time goes:
time: 247 us
  waiting for transfers between devices  112 us (45%)
  blocking collectives  52.8 us (21%)
  matrix products  52.5 us (21%)
  between operations  13.6 us (6%)
  local copies, waits for them, and re-layouts  6.26 us (3%)
  other arithmetic  6.03 us (2%)
  starting transfers between devices  3.55 us (1%)
    reduce_scatter x1, waiting for transfers between devices, body(): lax.psum_scatter((term * down_gain[:, None]).astype(jnp.bfloat16), 'tenso...  66.1 us
    psum x1, blocking collectives, body(): selected = lax.psum(selected, 'tensor')  35.8 us
    all_gather x1, waiting for transfers between devices, body(): piece = lax.all_gather(arrived, 'tensor', axis=1, tiled=True)  33.4 us
    dot_general x1, matrix products, body(): lax.dot_general(down_weight, hidden, (((0,), (1,)), ((), ())), preferred_...  28.4 us
    all_to_all x1, blocking collectives, body(): lax.all_to_all(outgoing, 'expert', split_axis=0, concat_axis=0, tiled=True)  17 us
    dot_general x1, matrix products, body(): up_next = jnp.dot(piece, up_weight, preferred_element_type=jnp.float32)  14.6 us
    all_to_all x1, waiting for transfers between devices, body(): lax.all_to_all(summed.reshape(width_part, expert_count, capacity), 'exper...  12.2 us
  transfers between devices with their start and end apart: 3, of which 3 were waited for; matrix products, arithmetic and copies ran while one was open for 4% of the time, Pallas kernels for 0%

commit v1 on v0

--- a/solution.py
+++ b/solution.py
@@ -1,6 +1,8 @@
 import jax
 import jax.numpy as jnp
 from jax import lax
+from jax.experimental import pallas as pl
+from jax.experimental.pallas import tpu as pltpu
 from jax.sharding import PartitionSpec as P
 
 ADAPTER_RANK = 64
@@ -147,9 +149,334 @@
     return output.astype(jnp.bfloat16)
 
 
+MESH_ID = pl.DeviceIdType.MESH
+
+
+def rcopy(src, dst, send, recv, device):
+    return pltpu.make_async_remote_copy(
+        src_ref=src, dst_ref=dst, send_sem=send, recv_sem=recv, device_id=device, device_id_type=MESH_ID
+    )
+
+
+def layer_kernel(
+    tok, meta, pt, ain, aout, gs, us, ds, wg, wu, wd, out,
+    X, wbuf, wdb, acc, hid, lat_s, lat_r, spread, pbuf, wrow, part, rs_buf, rx_buf, rz_buf,
+    local_sem, w_sem, wd_sem, x_recv, z_send, x_send, sib_send, fwd_send,
+    p_send, p_recv, lat_send, lat_recv, ps_send, ps_recv, px_send, px_recv, pz_send, pz_recv,
+):
+    rows, width = tok.shape
+    hidden = wbuf.shape[3]
+    all_rows = 4 * rows
+    g, e, z = lax.axis_index("groups"), lax.axis_index("expert"), lax.axis_index("tensor")
+    core = e % 2
+    e1 = e + 1 - 2 * core
+    e2 = (e + 2) % 4
+    e3 = (e1 + 2) % 4
+    pair_x, pair_own = 1 - e // 2, e // 2
+    h = z // 2
+    zz = z * (1 - h) + (3 - z) * h
+    order = [b * (1 - h) + (3 - b) * h for b in (zz, 1 - zz, 2, 3)]
+    inner = z + 1 - 2 * h
+    outer = (z - 1 + 2 * h + 4) % 4
+    others_e = (e1, e2, e3)
+    others_z = tuple((z + d) % 4 for d in (1, 2, 3))
+
+    def wload(k):
+        s, slot = order[k], k % 2
+        at = pl.ds(pl.multiple_of(s * width, width), width)
+        return [
+            pltpu.make_async_copy(w.at[at, :], wbuf.at[slot, i], w_sem.at[slot, i])
+            for i, w in enumerate((wg, wu))
+        ]
+
+    def wdload(i):
+        s = order[3 - i]
+        return pltpu.make_async_copy(
+            wd.at[:, pl.ds(pl.multiple_of(s * width, width), width)], wdb.at[i], wd_sem.at[i]
+        )
+
+    for k in (0, 1):
+        for c in wload(k):
+            c.start()
+    barrier = pltpu.get_barrier_semaphore()
+    for o in others_e:
+        pl.semaphore_signal(barrier, inc=1, device_id=(g, o, z), device_id_type=MESH_ID)
+    for o in others_z:
+        pl.semaphore_signal(barrier, inc=1, device_id=(g, e, o), device_id_type=MESH_ID)
+    pl.semaphore_wait(barrier, 6)
+
+    def to_z(k, target, send_index, src=None):
+        s = order[k]
+        return rcopy(X.at[s, e] if src is None else src, X.at[s, e], z_send.at[send_index], x_recv.at[s, e], (g, e, target))
+
+    def to_x(k, src=None):
+        s = order[k]
+        return rcopy(X.at[s, e] if src is None else src, X.at[s, e], x_send.at[k], x_recv.at[s, e], (g, e2, z))
+
+    def to_sib(k, src=None):
+        s = order[k]
+        return rcopy(X.at[s, e] if src is None else src, X.at[s, e], sib_send.at[k], x_recv.at[s, e], (g, e1, z))
+
+    def fwd_sib(k):
+        s = order[k]
+        return rcopy(X.at[s, e2], X.at[s, e2], fwd_send.at[k], x_recv.at[s, e2], (g, e1, z))
+
+    def arrived(k, b):
+        s = order[k]
+        rcopy(X.at[s, b], X.at[s, b], x_send.at[k], x_recv.at[s, b], (g, e2, z)).wait_recv()
+
+    p_copies = [rcopy(pt, pbuf.at[e], p_send.at[i], p_recv.at[e], (g, o, z)) for i, o in enumerate(others_e)]
+
+    to_x(0, tok).start()
+    to_z(0, inner, 0, tok).start()
+
+    @pl.when(zz == 1)
+    def _():
+        to_z(0, outer, 4, tok).start()
+
+    to_sib(0, tok).start()
+    for c in p_copies:
+        c.start()
+    for i in range(4):
+        wdload(i).start()
+    own = pltpu.make_async_copy(tok, X.at[z, e], local_sem)
+    own.start()
+    own.wait()
+
+    def forward(k):
+        arrived(k, e)
+
+        @pl.when(zz == 1)
+        def _():
+            to_z(k, inner if k == 1 else outer, k).start()
+
+        to_x(k).start()
+        to_sib(k).start()
+
+    lane = lax.broadcasted_iota(jnp.int32, (all_rows, 128), 1)
+    lat_copies = [
+        rcopy(lat_s, lat_r.at[z], lat_send.at[i], lat_recv.at[z], (g, e, o)) for i, o in enumerate(others_z)
+    ]
+
+    for k in range(4):
+        s, slot = order[k], k % 2
+        if k == 0:
+            forward(1)
+        if k < 2:
+            @pl.when(zz == 1)
+            def _():
+                forward(k + 2)
+
+            @pl.when(zz == 0)
+            def _():
+                if k > 0:
+                    forward(k + 1)
+        if k == 2:
+            @pl.when(zz == 0)
+            def _():
+                forward(3)
+        arrived(k, e2)
+        fwd_sib(k).start()
+        arrived(k, e1)
+        arrived(k, e3)
+        if k == 0:
+            a = meta[:, 2:3]
+            keep = jnp.where(lane < 64, 1.0 - a, a)
+            mixed = jnp.dot(X[s].reshape(all_rows, width), ain[...], preferred_element_type=jnp.float32)
+            m0, m1 = mixed[:, :128] * keep, mixed[:, 128:] * keep
+            m0 = m0 + pltpu.roll(m0, 64, 1)
+            m1 = m1 + pltpu.roll(m1, 64, 1)
+            lat_s[...] = jnp.where(lane < 64, m0, m1).astype(jnp.bfloat16)
+            for c in lat_copies:
+                c.start()
+            pbuf[e] = pt[...]
+        if k == 2:
+            for o in others_e:
+                rcopy(pt, pbuf.at[o], p_send.at[0], p_recv.at[o], (g, e2, z)).wait_recv()
+            for b in range(4):
+                p = pbuf[b].T
+                m = meta[b * rows:(b + 1) * rows, :]
+                w = p[:rows, 0:1] * m[:, 0:1] + p[:rows, 1:2] * m[:, 1:2]
+                wrow[b // 2, (b % 2) * rows:(b % 2 + 1) * rows, :] = jnp.broadcast_to(w, (rows, 128))
+        if k == 3:
+            for o in others_z:
+                rcopy(lat_s, lat_r.at[o], lat_send.at[0], lat_recv.at[o], (g, e, inner)).wait_recv()
+            total = lat_s[...].astype(jnp.float32)
+            for o in others_z:
+                total = total + lat_r[o].astype(jnp.float32)
+            a = meta[:, 2:3]
+            keep = jnp.where(lane < 64, 1.0 - a, a)
+            turned = pltpu.roll(total, 64, 1)
+            spread[0] = (jnp.where(lane < 64, total, turned) * keep).astype(jnp.bfloat16)
+            spread[1] = (jnp.where(lane < 64, turned, total) * keep).astype(jnp.bfloat16)
+        for c in wload(k):
+            c.wait()
+
+        if k < 3:
+            @pl.loop(0, hidden // 256)
+            def _(j):
+                at = pl.ds(pl.multiple_of(j * 256, 256), 256)
+                for i in range(2):
+                    d = jnp.dot(
+                        X[s].reshape(all_rows, width), wbuf[slot, i, :, at], preferred_element_type=jnp.float32
+                    )
+                    if k == 0:
+                        acc[i, :, at] = d
+                    else:
+                        acc[i, :, at] += d
+        else:
+            @pl.loop(0, hidden // 256)
+            def _(j):
+                at = pl.ds(pl.multiple_of(j * 256, 256), 256)
+                x = X[s].reshape(all_rows, width)
+                v = acc[0, :, at] + jnp.dot(x, wbuf[slot, 0, :, at], preferred_element_type=jnp.float32)
+                u = acc[1, :, at] + jnp.dot(x, wbuf[slot, 1, :, at], preferred_element_type=jnp.float32)
+                v = v * gs[:, at] + jnp.dot(spread[0], aout[0, :, at], preferred_element_type=jnp.float32)
+                u = u * us[:, at] + jnp.dot(spread[1], aout[1, :, at], preferred_element_type=jnp.float32)
+                y = (v / (1.0 + jnp.exp(-v)) * u).astype(jnp.bfloat16)
+                hid[:, :, at] = y.reshape(2, 2 * rows, 256)
+        if k < 2:
+            for c in wload(k + 2):
+                c.start()
+
+    def s_copy(n, i):
+        return rcopy(part.at[n, i, 1 - core], rs_buf.at[n, i], ps_send.at[n, i], ps_recv.at[n, i], (g, e1, z))
+
+    def x_copy(i):
+        return rcopy(part.at[0, i, core], rx_buf.at[i], px_send.at[i], px_recv.at[i], (g, e2, z))
+
+    def z_copy(i):
+        return rcopy(part.at[1, i, core], rz_buf.at[z], pz_send.at[i], pz_recv.at[z], (g, e, order[3 - i]))
+
+    def down(n, i):
+        pair = (pair_x, pair_own)[n]
+        s = order[3 - i]
+        if n == 0:
+            wdload(i).wait()
+
+        @pl.loop(0, width // 256)
+        def _(j):
+            at = pl.ds(pl.multiple_of(j * 256, 256), 256)
+            d = jnp.dot(hid[pair], wdb[i, :, at], preferred_element_type=jnp.float32)
+            d = d * ds[pl.ds(s, 1), at] * wrow[pair, :, 0:1]
+            part[n, i, :, :, at] = d.astype(jnp.bfloat16).reshape(2, rows, 256)
+        s_copy(n, i).start()
+
+    def send_x(i):
+        s_copy(0, i).wait_recv()
+        part[0, i, core] = (part[0, i, core].astype(jnp.float32) + rs_buf[0, i].astype(jnp.float32)).astype(
+            jnp.bfloat16
+        )
+        x_copy(i).start()
+
+    def gathered(i):
+        s_copy(1, i).wait_recv()
+        x_copy(i).wait_recv()
+        return (
+            part[1, i, core].astype(jnp.float32)
+            + rs_buf[1, i].astype(jnp.float32)
+            + rx_buf[i].astype(jnp.float32)
+        )
+
+    for i in range(4):
+        down(0, i)
+        if i > 0:
+            send_x(i - 1)
+    for i in range(4):
+        down(1, i)
+        if i == 0:
+            send_x(3)
+    for i in range(3):
+        part[1, i, core] = gathered(i).astype(jnp.bfloat16)
+        z_copy(i).start()
+    total = gathered(3)
+    for o in others_z:
+        rcopy(rz_buf.at[o], rz_buf.at[o], pz_send.at[0], pz_recv.at[o], (g, e, inner)).wait_recv()
+        total = total + rz_buf[o].astype(jnp.float32)
+    out[...] = total.astype(jnp.bfloat16)
+
+    to_z(0, inner, 0, tok).wait_send()
+
+    @pl.when(zz == 1)
+    def _():
+        to_z(0, outer, 4, tok).wait_send()
+        for k in (1, 2, 3):
+            to_z(k, inner if k == 1 else outer, k).wait_send()
+
+    for k in range(4):
+        to_x(k).wait_send()
+        to_sib(k).wait_send()
+        fwd_sib(k).wait_send()
+        x_copy(k).wait_send()
+        for n in range(2):
+            s_copy(n, k).wait_send()
+    for c in p_copies + lat_copies:
+        c.wait_send()
+    for i in range(3):
+        z_copy(i).wait_send()
+
+
+def fused_body(
+    tokens, routes, probs, request_adapter, gate_quant_levels, up_quant_levels, down_quant_levels,
+    gate_column_scale, up_column_scale, down_column_scale, adapter_input_maps, adapter_output_maps,
+):
+    rows, width = tokens.shape
+    hidden = gate_quant_levels.shape[2]
+    all_rows = routes.shape[0]
+    e = lax.axis_index("expert")
+    per = all_rows // request_adapter.shape[0]
+    adapter = jnp.broadcast_to(request_adapter[:, None], (request_adapter.shape[0], per)).reshape(-1, 1)
+    meta = jnp.concatenate(
+        [(routes == e).astype(jnp.float32), adapter.astype(jnp.float32), jnp.zeros((all_rows, 125), jnp.float32)],
+        axis=1,
+    )
+    pt = jnp.pad(probs.T, ((0, 6), (0, 256 - rows)))
+    ds = down_column_scale.reshape(4, width)
+    vm = pl.BlockSpec(memory_space=pltpu.VMEM)
+    hbm = pl.BlockSpec(memory_space=pl.ANY)
+    bf, f32 = jnp.bfloat16, jnp.float32
+    dma = pltpu.SemaphoreType.DMA
+    return pl.pallas_call(
+        layer_kernel,
+        out_shape=jax.ShapeDtypeStruct((rows, width), bf),
+        in_specs=[vm] * 8 + [hbm] * 3,
+        out_specs=vm,
+        scratch_shapes=[
+            pltpu.VMEM((4, 4, rows, width), bf),
+            pltpu.VMEM((2, 2, width, hidden), bf),
+            pltpu.VMEM((4, hidden, width), bf),
+            pltpu.VMEM((2, all_rows, hidden), f32),
+            pltpu.VMEM((2, 2 * rows, hidden), bf),
+            pltpu.VMEM((all_rows, 128), bf),
+            pltpu.VMEM((4, all_rows, 128), bf),
+            pltpu.VMEM((2, all_rows, 128), bf),
+            pltpu.VMEM((4, 8, 256), f32),
+            pltpu.VMEM((2, 2 * rows, 128), f32),
+            pltpu.VMEM((2, 4, 2, rows, width), bf),
+            pltpu.VMEM((2, 4, rows, width), bf),
+            pltpu.VMEM((4, rows, width), bf),
+            pltpu.VMEM((4, rows, width), bf),
+            dma, dma((2, 2)), dma((4,)), dma((4, 4)), dma((5,)), dma((4,)), dma((4,)), dma((4,)),
+            dma((3,)), dma((4,)), dma((3,)), dma((4,)), dma((2, 4)), dma((2, 4)), dma((4,)), dma((4,)),
+            dma((3,)), dma((4,)),
+        ],
+        compiler_params=pltpu.CompilerParams(
+            collective_id=0, has_side_effects=True, vmem_limit_bytes=63 * 1024 * 1024
+        ),
+        cost_estimate=pl.CostEstimate(
+            flops=6 * all_rows * 4 * width * hidden, bytes_accessed=6 * 4 * width * hidden, transcendentals=0
+        ),
+        name="moe_layer",
+    )(
+        tokens, meta, pt, adapter_input_maps[0], adapter_output_maps[0], gate_column_scale, up_column_scale, ds,
+        gate_quant_levels[0], up_quant_levels[0], down_quant_levels[0],
+    )
+
+
 def solution(mesh):
+    small = mesh.shape["expert"] == 4 and mesh.shape["tensor"] == 4
     return jax.shard_map(
-        body,
+        fused_body if small else body,
         mesh=mesh,
         in_specs=(
             P(("groups", "expert"), "tensor"),

time: 247 us -> 110 us (0.45)
  the two profiles are of different devices: /device:TPU:0 before, /device:TPU:11 now
where the time goes in v1:
time: 110 us; the launch traced here: 109 us
  Pallas kernels  101 us (92%)
  local copies, waits for them, and re-layouts  4.69 us (4%)
  other arithmetic  3.65 us (3%)
    pallas_call x1, Pallas kernels, fused_body(): pl.pallas_call(layer_kernel, out_shape=jax.ShapeDtypeStruct((rows, width)...  101 us
    unnamed x2, local copies, waits for them, and re-layouts  2.21 us

profile of v1, /device:TPU:11, one launch (start us, length us, event | category | flops | bytes accessed | tf_op | source)
XLA Modules:
  0.0 109.2 jit_solution(10212295302071643170)
XLA Ops:
  0.0 0.7 compare_convert_fusion
  0.7 0.2 copy.18
  0.9 0.7 convert_element_type.21
  1.6 0.1 broadcast_in_dim.4
  1.6 0.3 convert_element_type.23
  1.9 0.1 pad.7.clone
  2.0 0.9 maximum_maximum_fusion.meta
  2.9 0.5 broadcast.9
  3.4 1.4 %reduce.3 = f32[3072]{0:T(1024)S(1)} reduce(f32[1,3072]{1,0:T(1,128)} %param.21, f32[]{:T(128)} %broadcast.9), dimensions={0}, to_apply=%param.21.reduce_sub_computation.3 | reduce | bytes 24580 | tf_op args[9]
  4.8 0.6 reshape.18.ds
  5.4 1.3 %pad.4.pt = f32[8,256]{1,0:T(8,128)} pad(f32[2,192]{1,0:T(2,128)} %bitcast.6, f32[]{:T(128)} %constant.8.clone.1), padding=0_6x0_64 | pad | bytes 9732 | tf_op jit(solution)/shard_map/jit(_pad)/pad | solution.py:433
  6.7 100.8 %moe_layer.1 = bf16[192,768]{1,0:T(8,128)(2,1)} custom-call(bf16[192,768]{1,0:T(8,128)(2,1)} %tok.1, f32[768,128]{1,0:T(8,128)} %maximum_maximum_fusion.meta, f32[8,256]{1,0:T(8,128)} %pad.4.pt, bf16[768,256]{1,0:T(8,128)(2,1)} %bitcast.11, bf16[2,128,2048]{2,1,0:T(8,128)(2,1)} %bitcast.10, f32[1,2048]{1,0:T(1,128)} %gs.1, f32[1,2048]{1,0:T(1,128)} %us.1, ...), custom_call_target="tpu_custom_call" | custom-call | flops 28991029248 | bytes 37748736 | tf_op jit(solution)/shard_map/moe_layer/pallas_call | solution.py:439
  107.5 1.7 %copy.21 = bf16[192,768]{1,0:T(8,128)(2,1)} copy(bf16[192,768]{1,0:T(8,128)(2,1)} %moe_layer.1) | data formatting | bytes 589824
  (1 shorter events, 0.0 us)

commit v2 on v1

--- a/solution.py
+++ b/solution.py
@@ -159,10 +159,10 @@
 
 
 def layer_kernel(
-    tok, meta, pt, ain, aout, gs, us, ds, wg, wu, wd, out,
-    X, wbuf, wdb, acc, hid, lat_s, lat_r, spread, pbuf, wrow, part, rs_buf, rx_buf, rz_buf,
+    req, tok, routes, probs, ain, aout, gs, us, ds, wg, wu, wd, out,
+    X, wbuf, wdb, acc, hid, lat_s, lat_r, lat_t, spread, keep_s, turn_s, pt, pbuf, wrow, part, rs_buf, rx_buf, rz_buf,
     local_sem, w_sem, wd_sem, x_recv, z_send, x_send, sib_send, fwd_send,
-    p_send, p_recv, lat_send, lat_recv, ps_send, ps_recv, px_send, px_recv, pz_send, pz_recv,
+    p_send, p_recv, lat_send, lat_recv, lt_send, lt_recv, ps_send, ps_recv, px_send, px_recv, pz_send, pz_recv,
 ):
     rows, width = tok.shape
     hidden = wbuf.shape[3]
@@ -225,6 +225,11 @@
         s = order[k]
         rcopy(X.at[s, b], X.at[s, b], x_send.at[k], x_recv.at[s, b], (g, e2, z)).wait_recv()
 
+    turn_s[...] = jnp.zeros_like(turn_s)
+    turn_s[:rows, 0:2] = probs[...]
+    pt[...] = turn_s[...].T[:8]
+    pbuf[e] = pt[...]
+    lane = lax.broadcasted_iota(jnp.int32, (all_rows, 128), 1)
     p_copies = [rcopy(pt, pbuf.at[e], p_send.at[i], p_recv.at[e], (g, o, z)) for i, o in enumerate(others_e)]
 
     to_x(0, tok).start()
@@ -253,9 +258,18 @@
         to_x(k).start()
         to_sib(k).start()
 
-    lane = lax.broadcasted_iota(jnp.int32, (all_rows, 128), 1)
+    requests = req.shape[0]
+    per = all_rows // requests
+    row = lax.broadcasted_iota(jnp.int32, (all_rows, 128), 0)
+    chosen = jnp.zeros((all_rows, 128), jnp.int32)
+    for i in range(requests):
+        chosen = jnp.where((row >= i * per) & (row < (i + 1) * per), req[i], chosen)
+    keep_s[...] = jnp.where(chosen == jnp.where(lane < 64, 0, 1), 1.0, 0.0)
     lat_copies = [
-        rcopy(lat_s, lat_r.at[z], lat_send.at[i], lat_recv.at[z], (g, e, o)) for i, o in enumerate(others_z)
+        rcopy(lat_s.at[o], lat_r.at[z], lat_send.at[i], lat_recv.at[z], (g, e, o)) for i, o in enumerate(others_z)
+    ]
+    sum_copies = [
+        rcopy(lat_t.at[z], lat_t.at[z], lt_send.at[i], lt_recv.at[z], (g, e, o)) for i, o in enumerate(others_z)
     ]
 
     for k in range(4):
@@ -280,32 +294,36 @@
         arrived(k, e1)
         arrived(k, e3)
         if k == 0:
-            a = meta[:, 2:3]
-            keep = jnp.where(lane < 64, 1.0 - a, a)
+            keep = keep_s[...]
             mixed = jnp.dot(X[s].reshape(all_rows, width), ain[...], preferred_element_type=jnp.float32)
             m0, m1 = mixed[:, :128] * keep, mixed[:, 128:] * keep
             m0 = m0 + pltpu.roll(m0, 64, 1)
             m1 = m1 + pltpu.roll(m1, 64, 1)
-            lat_s[...] = jnp.where(lane < 64, m0, m1).astype(jnp.bfloat16)
+            lat_s[...] = jnp.where(lane < 64, m0, m1).astype(jnp.bfloat16).reshape(4, rows, 128)
+        if k == 1:
             for c in lat_copies:
                 c.start()
-            pbuf[e] = pt[...]
         if k == 2:
+            for o in others_z:
+                rcopy(lat_r.at[o], lat_r.at[o], lat_send.at[0], lat_recv.at[o], (g, e, inner)).wait_recv()
+            total = lat_s[z].astype(jnp.float32)
+            for o in others_z:
+                total = total + lat_r[o].astype(jnp.float32)
+            lat_t[z] = total.astype(jnp.bfloat16)
+            for c in sum_copies:
+                c.start()
             for o in others_e:
                 rcopy(pt, pbuf.at[o], p_send.at[0], p_recv.at[o], (g, e2, z)).wait_recv()
             for b in range(4):
                 p = pbuf[b].T
-                m = meta[b * rows:(b + 1) * rows, :]
+                m = jnp.where(routes[b * rows:(b + 1) * rows, :] == e, 1.0, 0.0)
                 w = p[:rows, 0:1] * m[:, 0:1] + p[:rows, 1:2] * m[:, 1:2]
                 wrow[b // 2, (b % 2) * rows:(b % 2 + 1) * rows, :] = jnp.broadcast_to(w, (rows, 128))
         if k == 3:
             for o in others_z:
-                rcopy(lat_s, lat_r.at[o], lat_send.at[0], lat_recv.at[o], (g, e, inner)).wait_recv()
-            total = lat_s[...].astype(jnp.float32)
-            for o in others_z:
-                total = total + lat_r[o].astype(jnp.float32)
-            a = meta[:, 2:3]
-            keep = jnp.where(lane < 64, 1.0 - a, a)
+                rcopy(lat_t.at[o], lat_t.at[o], lt_send.at[0], lt_recv.at[o], (g, e, inner)).wait_recv()
+            total = lat_t[...].reshape(all_rows, 128).astype(jnp.float32)
+            keep = keep_s[...]
             turned = pltpu.roll(total, 64, 1)
             spread[0] = (jnp.where(lane < 64, total, turned) * keep).astype(jnp.bfloat16)
             spread[1] = (jnp.where(lane < 64, turned, total) * keep).astype(jnp.bfloat16)
@@ -345,8 +363,13 @@
     def x_copy(i):
         return rcopy(part.at[0, i, core], rx_buf.at[i], px_send.at[i], px_recv.at[i], (g, e2, z))
 
-    def z_copy(i):
-        return rcopy(part.at[1, i, core], rz_buf.at[z], pz_send.at[i], pz_recv.at[z], (g, e, order[3 - i]))
+    def z_copy(i, middle):
+        target, slot = ((inner, 3), (inner, 4), (outer, 3))[i] if middle else (inner, 2 - i)
+        return rcopy(part.at[1, i, core], rz_buf.at[slot], pz_send.at[i], pz_recv.at[slot], (g, e, target))
+
+    def z_arrived(slot):
+        rcopy(rz_buf.at[slot], rz_buf.at[slot], pz_send.at[0], pz_recv.at[slot], (g, e, inner)).wait_recv()
+        return rz_buf[slot].astype(jnp.float32)
 
     def down(n, i):
         pair = (pair_x, pair_own)[n]
@@ -358,7 +381,7 @@
         def _(j):
             at = pl.ds(pl.multiple_of(j * 256, 256), 256)
             d = jnp.dot(hid[pair], wdb[i, :, at], preferred_element_type=jnp.float32)
-            d = d * ds[pl.ds(s, 1), at] * wrow[pair, :, 0:1]
+            d = d * ds[:, pl.ds(pl.multiple_of(s * width + j * 256, 256), 256)] * wrow[pair, :, 0:1]
             part[n, i, :, :, at] = d.astype(jnp.bfloat16).reshape(2, rows, 256)
         s_copy(n, i).start()
 
@@ -386,14 +409,19 @@
         down(1, i)
         if i == 0:
             send_x(3)
-    for i in range(3):
-        part[1, i, core] = gathered(i).astype(jnp.bfloat16)
-        z_copy(i).start()
-    total = gathered(3)
-    for o in others_z:
-        rcopy(rz_buf.at[o], rz_buf.at[o], pz_send.at[0], pz_recv.at[o], (g, e, inner)).wait_recv()
-        total = total + rz_buf[o].astype(jnp.float32)
-    out[...] = total.astype(jnp.bfloat16)
+    for middle in (False, True):
+        @pl.when(zz == int(middle))
+        def _():
+            for i in range(3):
+                total = gathered(i)
+                if middle:
+                    total = total + z_arrived((2, 1, 3)[i])
+                part[1, i, core] = total.astype(jnp.bfloat16)
+                z_copy(i, middle).start()
+            total = gathered(3)
+            for slot in (0, 4) if middle else (3,):
+                total = total + z_arrived(slot)
+            out[...] = total.astype(jnp.bfloat16)
 
     to_z(0, inner, 0, tok).wait_send()
 
@@ -410,10 +438,10 @@
         x_copy(k).wait_send()
         for n in range(2):
             s_copy(n, k).wait_send()
-    for c in p_copies + lat_copies:
+    for c in p_copies + lat_copies + sum_copies:
         c.wait_send()
     for i in range(3):
-        z_copy(i).wait_send()
+        z_copy(i, False).wait_send()
 
 
 def fused_body(
@@ -423,15 +451,6 @@
     rows, width = tokens.shape
     hidden = gate_quant_levels.shape[2]
     all_rows = routes.shape[0]
-    e = lax.axis_index("expert")
-    per = all_rows // request_adapter.shape[0]
-    adapter = jnp.broadcast_to(request_adapter[:, None], (request_adapter.shape[0], per)).reshape(-1, 1)
-    meta = jnp.concatenate(
-        [(routes == e).astype(jnp.float32), adapter.astype(jnp.float32), jnp.zeros((all_rows, 125), jnp.float32)],
-        axis=1,
-    )
-    pt = jnp.pad(probs.T, ((0, 6), (0, 256 - rows)))
-    ds = down_column_scale.reshape(4, width)
     vm = pl.BlockSpec(memory_space=pltpu.VMEM)
     hbm = pl.BlockSpec(memory_space=pl.ANY)
     bf, f32 = jnp.bfloat16, jnp.float32
@@ -439,7 +458,7 @@
     return pl.pallas_call(
         layer_kernel,
         out_shape=jax.ShapeDtypeStruct((rows, width), bf),
-        in_specs=[vm] * 8 + [hbm] * 3,
+        in_specs=[pl.BlockSpec(memory_space=pltpu.SMEM)] + [vm] * 8 + [hbm] * 3,
         out_specs=vm,
         scratch_shapes=[
             pltpu.VMEM((4, 4, rows, width), bf),
@@ -447,18 +466,22 @@
             pltpu.VMEM((4, hidden, width), bf),
             pltpu.VMEM((2, all_rows, hidden), f32),
             pltpu.VMEM((2, 2 * rows, hidden), bf),
-            pltpu.VMEM((all_rows, 128), bf),
-            pltpu.VMEM((4, all_rows, 128), bf),
+            pltpu.VMEM((4, rows, 128), bf),
+            pltpu.VMEM((4, rows, 128), bf),
+            pltpu.VMEM((4, rows, 128), bf),
             pltpu.VMEM((2, all_rows, 128), bf),
+            pltpu.VMEM((all_rows, 128), f32),
+            pltpu.VMEM((256, 128), f32),
+            pltpu.VMEM((8, 256), f32),
             pltpu.VMEM((4, 8, 256), f32),
             pltpu.VMEM((2, 2 * rows, 128), f32),
             pltpu.VMEM((2, 4, 2, rows, width), bf),
             pltpu.VMEM((2, 4, rows, width), bf),
             pltpu.VMEM((4, rows, width), bf),
-            pltpu.VMEM((4, rows, width), bf),
+            pltpu.VMEM((5, rows, width), bf),
             dma, dma((2, 2)), dma((4,)), dma((4, 4)), dma((5,)), dma((4,)), dma((4,)), dma((4,)),
-            dma((3,)), dma((4,)), dma((3,)), dma((4,)), dma((2, 4)), dma((2, 4)), dma((4,)), dma((4,)),
-            dma((3,)), dma((4,)),
+            dma((3,)), dma((4,)), dma((3,)), dma((4,)), dma((3,)), dma((4,)), dma((2, 4)), dma((2, 4)),
+            dma((4,)), dma((4,)), dma((3,)), dma((5,)),
         ],
         compiler_params=pltpu.CompilerParams(
             collective_id=0, has_side_effects=True, vmem_limit_bytes=63 * 1024 * 1024
@@ -468,7 +491,8 @@
         ),
         name="moe_layer",
     )(
-        tokens, meta, pt, adapter_input_maps[0], adapter_output_maps[0], gate_column_scale, up_column_scale, ds,
+        request_adapter, tokens, routes, probs, adapter_input_maps[0], adapter_output_maps[0],
+        gate_column_scale, up_column_scale, down_column_scale,
         gate_quant_levels[0], up_quant_levels[0], down_quant_levels[0],
     )
 

time: 110 us -> 98.6 us (0.90)
  the two profiles are of different devices: /device:TPU:11 before, /device:TPU:0 now
where the time goes in v2:
time: 98.6 us; the launch traced here: 98.4 us
  Pallas kernels  93.6 us (95%)
  local copies, waits for them, and re-layouts  4.75 us (5%)
    pallas_call x1, Pallas kernels, fused_body(): pl.pallas_call(layer_kernel, out_shape=jax.ShapeDtypeStruct((rows, width)...  93.6 us
    unnamed x3, local copies, waits for them, and re-layouts  4.75 us

profile of v2, /device:TPU:0, one launch (start us, length us, event | category | flops | bytes accessed | tf_op | source)
XLA Modules:
  0.0 98.4 jit_solution(8702641768016888714)
XLA Ops:
  0.0 1.4 %copy.14.probs = f32[192,2]{1,0:T(8,128)} copy(f32[192,2]{0,1:T(2,128)} %param.14) | data formatting | bytes 3072 | tf_op args[2]
  1.4 1.6 %copy.13.routes = s32[768,2]{1,0:T(8,128)} copy(s32[768,2]{0,1:T(2,128)} %param.13) | data formatting | bytes 12288 | tf_op args[1]
  3.1 93.6 %moe_layer.1 = bf16[192,768]{1,0:T(8,128)(2,1)} custom-call(s32[8]{0:T(128)} %req.1, bf16[192,768]{1,0:T(8,128)(2,1)} %tok.1, s32[768,2]{1,0:T(8,128)} %copy.13.routes, f32[192,2]{1,0:T(8,128)} %copy.14.probs, bf16[768,256]{1,0:T(8,128)(2,1)} %bitcast.9, bf16[2,128,2048]{2,1,0:T(8,128)(2,1)} %bitcast.8, f32[1,2048]{1,0:T(1,128)} %gs.1, f32[1,2048]{1,0:T(1,128)} %us.1, ...), custom_call_target="tpu_custom_call" | custom-call | flops 28991029248 | bytes 37748736 | tf_op jit(solution)/shard_map/moe_layer/pallas_call | solution.py:458
  96.7 1.7 %copy.16 = bf16[192,768]{1,0:T(8,128)(2,1)} copy(bf16[192,768]{1,0:T(8,128)(2,1)} %moe_layer.1) | data formatting | bytes 589824

commit v3 on v2

--- a/solution.py
+++ b/solution.py
@@ -226,8 +226,8 @@
         rcopy(X.at[s, b], X.at[s, b], x_send.at[k], x_recv.at[s, b], (g, e2, z)).wait_recv()
 
     turn_s[...] = jnp.zeros_like(turn_s)
-    turn_s[:rows, 0:2] = probs[...]
-    pt[...] = turn_s[...].T[:8]
+    pt[...] = jnp.zeros_like(pt)
+    pt[0:2, 0:rows] = probs[...]
     pbuf[e] = pt[...]
     lane = lax.broadcasted_iota(jnp.int32, (all_rows, 128), 1)
     p_copies = [rcopy(pt, pbuf.at[e], p_send.at[i], p_recv.at[e], (g, o, z)) for i, o in enumerate(others_e)]
@@ -315,9 +315,10 @@
             for o in others_e:
                 rcopy(pt, pbuf.at[o], p_send.at[0], p_recv.at[o], (g, e2, z)).wait_recv()
             for b in range(4):
-                p = pbuf[b].T
-                m = jnp.where(routes[b * rows:(b + 1) * rows, :] == e, 1.0, 0.0)
-                w = p[:rows, 0:1] * m[:, 0:1] + p[:rows, 1:2] * m[:, 1:2]
+                m = jnp.where(routes[:, b * rows:(b + 1) * rows] == e, 1.0, 0.0)
+                turn_s[0:2, 0:rows] = pbuf[b, 0:2, 0:rows] * m
+                w = turn_s[...].T
+                w = w[:rows, 0:1] + w[:rows, 1:2]
                 wrow[b // 2, (b % 2) * rows:(b % 2 + 1) * rows, :] = jnp.broadcast_to(w, (rows, 128))
         if k == 3:
             for o in others_z:
@@ -325,34 +326,24 @@
             total = lat_t[...].reshape(all_rows, 128).astype(jnp.float32)
             keep = keep_s[...]
             turned = pltpu.roll(total, 64, 1)
-            spread[0] = (jnp.where(lane < 64, total, turned) * keep).astype(jnp.bfloat16)
-            spread[1] = (jnp.where(lane < 64, turned, total) * keep).astype(jnp.bfloat16)
+            spread[0] = (jnp.where(lane < 64, total, turned) * keep).astype(jnp.bfloat16).reshape(2, 2 * rows, 128)
+            spread[1] = (jnp.where(lane < 64, turned, total) * keep).astype(jnp.bfloat16).reshape(2, 2 * rows, 128)
         for c in wload(k):
             c.wait()
 
         if k < 3:
-            @pl.loop(0, hidden // 256)
+            @pl.loop(0, hidden // 512)
             def _(j):
-                at = pl.ds(pl.multiple_of(j * 256, 256), 256)
+                at = pl.ds(pl.multiple_of(j * 512, 512), 512)
                 for i in range(2):
                     d = jnp.dot(
                         X[s].reshape(all_rows, width), wbuf[slot, i, :, at], preferred_element_type=jnp.float32
                     )
+                    d = d.reshape(2, 2 * rows, 512)
                     if k == 0:
-                        acc[i, :, at] = d
+                        acc[i, :, :, at] = d
                     else:
-                        acc[i, :, at] += d
-        else:
-            @pl.loop(0, hidden // 256)
-            def _(j):
-                at = pl.ds(pl.multiple_of(j * 256, 256), 256)
-                x = X[s].reshape(all_rows, width)
-                v = acc[0, :, at] + jnp.dot(x, wbuf[slot, 0, :, at], preferred_element_type=jnp.float32)
-                u = acc[1, :, at] + jnp.dot(x, wbuf[slot, 1, :, at], preferred_element_type=jnp.float32)
-                v = v * gs[:, at] + jnp.dot(spread[0], aout[0, :, at], preferred_element_type=jnp.float32)
-                u = u * us[:, at] + jnp.dot(spread[1], aout[1, :, at], preferred_element_type=jnp.float32)
-                y = (v / (1.0 + jnp.exp(-v)) * u).astype(jnp.bfloat16)
-                hid[:, :, at] = y.reshape(2, 2 * rows, 256)
+                        acc[i, :, :, at] += d
         if k < 2:
             for c in wload(k + 2):
                 c.start()
@@ -377,12 +368,12 @@
         if n == 0:
             wdload(i).wait()
 
-        @pl.loop(0, width // 256)
+        @pl.loop(0, width // 768)
         def _(j):
-            at = pl.ds(pl.multiple_of(j * 256, 256), 256)
+            at = pl.ds(pl.multiple_of(j * 768, 768), 768)
             d = jnp.dot(hid[pair], wdb[i, :, at], preferred_element_type=jnp.float32)
-            d = d * ds[:, pl.ds(pl.multiple_of(s * width + j * 256, 256), 256)] * wrow[pair, :, 0:1]
-            part[n, i, :, :, at] = d.astype(jnp.bfloat16).reshape(2, rows, 256)
+            d = d * ds[:, pl.ds(pl.multiple_of(s * width + j * 768, 768), 768)] * wrow[pair, :, 0:1]
+            part[n, i, :, :, at] = d.astype(jnp.bfloat16).reshape(2, rows, 768)
         s_copy(n, i).start()
 
     def send_x(i):
@@ -401,14 +392,28 @@
             + rx_buf[i].astype(jnp.float32)
         )
 
+    def finish(pair):
+        s, slot = order[3], 1
+
+        @pl.loop(0, hidden // 512)
+        def _(j):
+            at = pl.ds(pl.multiple_of(j * 512, 512), 512)
+            x = X[s, pl.ds(pair * 2, 2)].reshape(2 * rows, width)
+            v = acc[0, pair, :, at] + jnp.dot(x, wbuf[slot, 0, :, at], preferred_element_type=jnp.float32)
+            u = acc[1, pair, :, at] + jnp.dot(x, wbuf[slot, 1, :, at], preferred_element_type=jnp.float32)
+            v = v * gs[:, at] + jnp.dot(spread[0, pair], aout[0, :, at], preferred_element_type=jnp.float32)
+            u = u * us[:, at] + jnp.dot(spread[1, pair], aout[1, :, at], preferred_element_type=jnp.float32)
+            hid[pair, :, at] = (v / (1.0 + jnp.exp(-v)) * u).astype(jnp.bfloat16)
+
+    finish(pair_x)
     for i in range(4):
         down(0, i)
         if i > 0:
             send_x(i - 1)
+    send_x(3)
+    finish(pair_own)
     for i in range(4):
         down(1, i)
-        if i == 0:
-            send_x(3)
     for middle in (False, True):
         @pl.when(zz == int(middle))
         def _():
@@ -464,14 +469,14 @@
             pltpu.VMEM((4, 4, rows, width), bf),
             pltpu.VMEM((2, 2, width, hidden), bf),
             pltpu.VMEM((4, hidden, width), bf),
-            pltpu.VMEM((2, all_rows, hidden), f32),
+            pltpu.VMEM((2, 2, 2 * rows, hidden), f32),
             pltpu.VMEM((2, 2 * rows, hidden), bf),
             pltpu.VMEM((4, rows, 128), bf),
             pltpu.VMEM((4, rows, 128), bf),
             pltpu.VMEM((4, rows, 128), bf),
-            pltpu.VMEM((2, all_rows, 128), bf),
+            pltpu.VMEM((2, 2, 2 * rows, 128), bf),
             pltpu.VMEM((all_rows, 128), f32),
-            pltpu.VMEM((256, 128), f32),
+            pltpu.VMEM((8, 256), f32),
             pltpu.VMEM((8, 256), f32),
             pltpu.VMEM((4, 8, 256), f32),
             pltpu.VMEM((2, 2 * rows, 128), f32),
@@ -491,7 +496,7 @@
         ),
         name="moe_layer",
     )(
-        request_adapter, tokens, routes, probs, adapter_input_maps[0], adapter_output_maps[0],
+        request_adapter, tokens, routes.T, probs.T, adapter_input_maps[0], adapter_output_maps[0],
         gate_column_scale, up_column_scale, down_column_scale,
         gate_quant_levels[0], up_quant_levels[0], down_quant_levels[0],
     )

time: 98.6 us -> 94.6 us (0.959)
  local copies, waits for them, and re-layouts: 4.75 us -> 1.69 us
    unnamed x3 -> x1, local copies, waits for them, and re-layouts: 4.75 us -> 1.69 us
where the time goes in v3:
time: 94.6 us; the launch traced here: 94.4 us
  Pallas kernels  92.7 us (98%)
  local copies, waits for them, and re-layouts  1.69 us (2%)
    pallas_call x1, Pallas kernels, fused_body(): pl.pallas_call(layer_kernel, out_shape=jax.ShapeDtypeStruct((rows, width)...  92.7 us

profile of v3, /device:TPU:0, one launch (start us, length us, event | category | flops | bytes accessed | tf_op | source)
XLA Modules:
  0.0 94.4 jit_solution(6350171809149941362)
XLA Ops:
  0.0 92.7 %moe_layer.1 = bf16[192,768]{1,0:T(8,128)(2,1)} custom-call(s32[8]{0:T(128)} %req.1, bf16[192,768]{1,0:T(8,128)(2,1)} %tok.1, s32[2,768]{1,0:T(2,128)} %bitcast.12, f32[2,192]{1,0:T(2,128)} %bitcast.13, bf16[768,256]{1,0:T(8,128)(2,1)} %bitcast.11, bf16[2,128,2048]{2,1,0:T(8,128)(2,1)} %bitcast.10, f32[1,2048]{1,0:T(1,128)} %gs.1, f32[1,2048]{1,0:T(1,128)} %us.1, ...), custom_call_target="tpu_custom_call" | custom-call | flops 28991029248 | bytes 37748736 | tf_op jit(solution)/shard_map/moe_layer/pallas_call | solution.py:463
  92.7 1.7 %copy.14 = bf16[192,768]{1,0:T(8,128)(2,1)} copy(bf16[192,768]{1,0:T(8,128)(2,1)} %moe_layer.1) | data formatting | bytes 589824
